TPU v7x, 32 devices: a whole 2x2x4 slice. The times are simulated.
32 devices in a mesh: groups: 1, epouter: 16 (over z, y, core), epinner: 2 (over x).
Axes of the slice: x: 2, y: 2, z: 4, core: 2. Of those that a mesh axis runs over, the one named last changes fastest.
Arguments:
- tokens: bfloat16 [1024, 7168], P(('groups', 'epouter'), 'epinner'), may hold values from -6 to 6
- expert_ids: int32 [1024, 2], P(('groups', 'epouter')), may hold values from 0 to 3, all different within a row; in each aligned block of 64 rows (0 to 63, 64 to 127, ...) at most 48 rows name the same one
- route_weight: float32 [1024, 2], P(('groups', 'epouter')), may hold values from 0.1 to 0.5
- w_gate: bfloat16 [16, 7168, 384], P('epouter', 'epinner'), may hold values from -0.0625 to 0.0625
- w_up: bfloat16 [16, 7168, 384], P('epouter', 'epinner'), may hold values from -0.0625 to 0.0625
- w_down: bfloat16 [16, 384, 7168], P('epouter', None, 'epinner'), may hold values from -0.15625 to 0.15625
Outputs:
- moe_out: bfloat16 [1024, 7168], P(('groups', 'epouter'), 'epinner')
Inputs may be any that keep to these rules, and one draw needn't show every extreme that they name: `expert_ids`: each row names 2 different experts; in each aligned block of 64 rows (the rows of one index of epouter) no expert is named by more than 48 rows, and in some block one expert is named by exactly 48 rows.
All inputs are finite; a program needn't handle non-finite values.
Results may differ from a plain program's by a relative error of at most 0.0058.
Values may be sent and summed in bfloat16 or wider, within the bound.
A program may use at most 64 MiB of HBM per device.

v0:
```python
import jax
import jax.numpy as jnp
from jax import lax
from jax.sharding import PartitionSpec as P

SLICES = 4


def place_matrix(flat_routes, experts, slot_depth):
    onehot = (flat_routes[:, None] == jnp.arange(experts, dtype=jnp.int32)[None, :]).astype(
        jnp.int32
    )
    before = jnp.cumsum(onehot, axis=0) - onehot
    slot_index = jnp.sum(before * onehot, axis=1)
    position = flat_routes * slot_depth + slot_index
    matches = position[None, :] == jnp.arange(experts * slot_depth, dtype=jnp.int32)[:, None]
    return (matches, position)


def dispatch_rows(matches, token_rows, picks):
    chosen = jnp.sum(
        matches.reshape(matches.shape[0], token_rows.shape[0], picks).astype(jnp.float32), axis=2
    )
    return jnp.dot(
        chosen.astype(jnp.bfloat16), token_rows, preferred_element_type=jnp.float32
    ).astype(jnp.bfloat16)


def spread_slices(packed, experts, slot_depth):
    row_width = packed.shape[1]
    widened = jnp.broadcast_to(
        packed.reshape(experts, 1, slot_depth, row_width), (experts, SLICES, slot_depth, row_width)
    )
    return widened.reshape(experts * SLICES, slot_depth, row_width)


def combine_rows(position, gate_values, returned, experts, picks):
    slot_depth = returned.shape[1]
    row_width = returned.shape[2]
    summed = jnp.sum(
        returned.reshape(experts, SLICES, slot_depth, row_width).astype(jnp.float32), axis=1
    )
    summed = summed.reshape(experts * slot_depth, row_width)
    fetched = jnp.take(summed, position, axis=0) * gate_values[:, None]
    return jnp.sum(fetched.reshape(-1, picks, row_width), axis=1)


def silu_product(gate_part, up_part):
    return (jax.nn.silu(gate_part) * up_part).astype(jnp.bfloat16)


def expert_rows(token_rows, weights):
    gate_matrix, up_matrix, down_matrix = weights
    gate_part = jnp.dot(token_rows, gate_matrix, preferred_element_type=jnp.float32)
    up_part = jnp.dot(token_rows, up_matrix, preferred_element_type=jnp.float32)
    gate_part, up_part = (
        lax.psum_scatter(gate_part, "epinner", scatter_dimension=0, tiled=True),
        lax.psum_scatter(up_part, "epinner", scatter_dimension=0, tiled=True),
    )
    hidden = lax.all_gather(silu_product(gate_part, up_part), "epinner", axis=0, tiled=True)
    return jnp.dot(hidden, down_matrix, preferred_element_type=jnp.float32).astype(jnp.bfloat16)


def shards(tokens, expert_ids, route_weight, w_gate, w_up, w_down):
    outer_size = lax.axis_size("epouter")
    experts = outer_size // SLICES
    block_count = tokens.shape[0]
    slice_width = tokens.shape[1]
    picks = expert_ids.shape[1]
    slot_depth = min(block_count, 3 * block_count * picks // (2 * experts))
    weights = (w_gate[0], w_up[0], w_down[0])
    matches, position = place_matrix(expert_ids.reshape(-1), experts, slot_depth)
    outgoing = spread_slices(dispatch_rows(matches, tokens, picks), experts, slot_depth)
    arrived = lax.all_to_all(outgoing, "epouter", split_axis=0, concat_axis=0, tiled=True)
    slot_count = arrived.shape[1]
    outputs = expert_rows(arrived.reshape(outer_size * slot_count, slice_width), weights)
    returned = lax.all_to_all(
        outputs.reshape(outer_size, slot_count, slice_width),
        "epouter",
        split_axis=0,
        concat_axis=0,
        tiled=True,
    )
    result = combine_rows(position, route_weight.reshape(-1), returned, experts, picks)
    return result.astype(jnp.bfloat16)


def solution(mesh):
    placed = (
        P(("groups", "epouter"), "epinner"),
        P(("groups", "epouter"), None),
        P(("groups", "epouter"), None),
        P("epouter", "epinner", None),
        P("epouter", "epinner", None),
        P("epouter", None, "epinner"),
    )
    return jax.shard_map(
        shards,
        mesh=mesh,
        in_specs=placed,
        out_specs=P(("groups", "epouter"), "epinner"),
        check_vma=False,
    )
```

profile of v0, /device:TPU:13, one launch (start us, length us, event | category | flops | bytes accessed | tf_op | source)
XLA Modules:
  0.0 359.0 jit_solution(2226919065568836392)
XLA Ops:
  6.5 0.0 copy-start
  6.5 0.0 reduce-scatter.3.cloned.1.call-start
  6.5 0.9 copy.17
  7.5 0.1 reshape.86
  7.6 0.1 fusion.5
  7.7 0.2 reduce_window_sum.11
  7.9 0.2 select_reduce_fusion
  8.0 0.1 reduce_sum.41
  8.2 0.1 copy.18
  8.3 0.7 compare_and_fusion
  9.0 0.1 convert_reduce_fusion.1
  9.1 1.6 convolution_convert_fusion.1
  10.6 0.5 broadcast_in_dim.22
  11.2 0.0 copy-start.4
  11.2 127.0 %all_to_all.10 = bf16[16,48,3584]{2,1,0:T(8,128)(2,1)S(1)} all-to-all(bf16[16,48,3584]{2,1,0:T(8,128)(2,1)S(1)} %bitcast.29), channel_id=1, replica_groups=mesh['groups'=1,'epouter'=16,'epinner'=2] {'epouter'}, dimensions={0} | all-to-all | bytes 11010048 | tf_op jit(solution)/shard_map/all_to_all | solution.py:74
  138.1 0.0 copy-start.1
  138.1 2.4 copy-done.1
  140.5 0.0 copy-done.4
  140.5 4.0 %fusion.3 = f32[768,384]{1,0:T(8,128)} fusion(bf16[768,3584]{1,0:T(8,128)(2,1)S(1)} %bitcast.31, bf16[1,3584,384]{2,1,0:T(8,128)(2,1)S(1)} %copy-done.4), kind=kOutput, calls=%fused_computation.7 | convolution fusion | flops 2113929216 | bytes 9437184 | tf_op jit(solution)/shard_map/dot_general | solution.py:54
  144.6 0.0 reduce-scatter.3.cloned.1.call-update
  144.6 0.0 reduce-scatter.5.cloned.1.call-start
  144.6 7.4 %fusion.1 = f32[768,384]{1,0:T(8,128)} fusion(bf16[768,3584]{1,0:T(8,128)(2,1)} %bitcast.32, bf16[1,3584,384]{2,1,0:T(8,128)(2,1)} %param.10), kind=kOutput, calls=%fused_computation.5 | convolution fusion | flops 2113929216 | bytes 9437184 | tf_op jit(solution)/shard_map/dot_general | solution.py:55
  152.0 0.0 reduce-scatter.5.cloned.1.call-update
  152.1 14.4 %reduce-scatter.3.cloned.1.call-done = f32[384,384]{1,0:T(8,128)} async-done(((f32[768,384]{1,0:T(8,128)}), f32[384,384]{1,0:T(8,128)}) %reduce-scatter.3.cloned.1.call-update) | async-done | bytes 589840 | tf_op jit(solution)/shard_map/reduce_scatter | solution.py:57
  166.5 24.1 %reduce-scatter.5.cloned.1.call-done = f32[384,384]{1,0:T(8,128)} async-done(((f32[768,384]{1,0:T(8,128)}), f32[384,384]{1,0:T(8,128)}) %reduce-scatter.5.cloned.1.call-update) | async-done | bytes 589840 | tf_op jit(solution)/shard_map/reduce_scatter | solution.py:58
  190.6 1.4 multiply_convert_fusion
  192.0 8.6 %all_gather.3 = bf16[768,384]{1,0:T(8,128)(2,1)S(1)} all-gather(bf16[384,384]{1,0:T(8,128)(2,1)S(1)} %multiply_convert_fusion), channel_id=1, replica_groups=mesh['groups'=1,'epouter'=16,'epinner'=2] {'epinner'}, dimensions={0}, use_global_device_ids=true | all-gather | bytes 884736 | tf_op jit(solution)/shard_map/all_gather | solution.py:60
  200.6 0.0 copy-done
  200.6 4.8 %convolution_convert_fusion = bf16[768,3584]{1,0:T(8,128)(2,1)} fusion(bf16[768,384]{1,0:T(8,128)(2,1)S(1)} %all_gather.3, bf16[1,384,3584]{2,1,0:T(8,128)(2,1)S(1)} %copy-done), kind=kOutput, calls=%fused_computation.2 | convolution fusion | flops 2116681728 | bytes 8847360 | tf_op jit(solution)/shard_map/dot_general | solution.py:61
  205.4 0.0 copy-start.2
  205.4 0.0 copy-start.3
  205.4 7.4 %all-to-all-start.1 = ((bf16[16,48,3584]{2,1,0:T(8,128)(2,1)}), bf16[16,48,3584]{2,1,0:T(8,128)(2,1)}, u32[]{:S(2)}, u32[]{:S(2)}) async-start(bf16[16,48,3584]{2,1,0:T(8,128)(2,1)} %bitcast.30), calls=%async_computation.3 | async-start | bytes 11010048 | tf_op jit(solution)/shard_map/all_to_all | solution.py:77
  212.7 0.0 copy-done.2
  212.8 0.1 copy.20
  212.9 0.1 mul.47
  213.0 0.1 copy.19
  213.1 0.0 copy-done.3
  213.1 0.1 copy.21
  213.2 120.1 %all-to-all-done.1 = bf16[16,48,3584]{2,1,0:T(8,128)(2,1)} async-done(((bf16[16,48,3584]{2,1,0:T(8,128)(2,1)}), bf16[16,48,3584]{2,1,0:T(8,128)(2,1)}, u32[]{:S(2)}, u32[]{:S(2)}) %all-to-all-start.1) | async-done | bytes 5505056 | tf_op jit(solution)/shard_map/all_to_all | solution.py:77
  333.3 5.2 %convert_reduce_fusion = f32[4,48,3584]{2,1,0:T(8,128)} fusion(bf16[16,48,3584]{2,1,0:T(8,128)(2,1)} %all-to-all-done.1), kind=kLoop, calls=%fused_computation.1 | loop fusion | flops 4816896 | bytes 8257536 | tf_op jit(solution)/shard_map/reduce_sum | solution.py:40
  338.5 5.0 %gather_fusion = f32[128,3584]{1,0:T(8,128)} fusion(f32[192,3584]{1,0:T(8,128)} %bitcast.28, s32[1024]{0:T(1024)S(1)} %pad_clamp_fusion), kind=kCustom, calls=%fused_computation | custom fusion | bytes 3670528 | tf_op jit(solution)/shard_map/jit(_take)/gather | solution.py:44
  343.5 3.3 gather.7
  346.7 5.4 %multiply_reduce_fusion = bf16[64,3584]{1,0:T(8,128)(2,1)} fusion(f32[64,2,3584]{2,1,0:T(2,128)} %gather.7, pred[64,2]{1,0:T(8,128)(4,1)S(1)} %copy.19, f32[64,2]{1,0:T(8,128)S(1)} %copy.21), kind=kLoop, calls=%fused_computation.9 | loop fusion | flops 1146880 | bytes 2294400 | tf_op jit(solution)/shard_map/reduce_sum | solution.py:45
  (3 shorter events, 0.0 us)
Async XLA Ops:
  6.5 194.1 %copy-start = (bf16[1,384,3584]{2,1,0:T(8,128)(2,1)S(1)}, bf16[1,384,3584]{2,1,0:T(8,128)(2,1)}, u32[]{:S(2)}) copy-start(bf16[1,384,3584]{2,1,0:T(8,128)(2,1)} %param.11) | copy-start | bytes 8257540
  6.5 159.9 %reduce-scatter.3.cloned.1.call-start = ((), (), s32[]{:S(2)}) async-start(), calls=%async_computation.4 | async-start | bytes 1769472 | tf_op jit(solution)/shard_map/reduce_scatter | solution.py:57
  11.2 129.4 %copy-start.4 = (bf16[1,3584,384]{2,1,0:T(8,128)(2,1)S(1)}, bf16[1,3584,384]{2,1,0:T(8,128)(2,1)}, u32[]{:S(2)}) copy-start(bf16[1,3584,384]{2,1,0:T(8,128)(2,1)} %param.9) | copy-start | bytes 8257540
  138.1 2.4 copy-start.1
  144.6 46.0 %reduce-scatter.5.cloned.1.call-start = ((), (), s32[]{:S(2)}) async-start(), calls=%async_computation.5 | async-start | bytes 1769472 | tf_op jit(solution)/shard_map/reduce_scatter | solution.py:58
  205.4 7.4 %copy-start.2 = (s32[64,2]{0,1:T(2,128)S(1)}, s32[64,2]{0,1:T(2,128)}, u32[]{:S(2)}) copy-start(s32[64,2]{0,1:T(2,128)} %param.7) | copy-start | bytes 1540
  205.4 7.7 %copy-start.3 = (f32[64,2]{0,1:T(2,128)S(1)}, f32[64,2]{0,1:T(2,128)}, u32[]{:S(2)}) copy-start(f32[64,2]{0,1:T(2,128)} %param.8) | copy-start | bytes 1540
  205.4 127.9 %all-to-all-start.1 = ((bf16[16,48,3584]{2,1,0:T(8,128)(2,1)}), bf16[16,48,3584]{2,1,0:T(8,128)(2,1)}, u32[]{:S(2)}, u32[]{:S(2)}) async-start(bf16[16,48,3584]{2,1,0:T(8,128)(2,1)} %bitcast.30), calls=%async_computation.3 | async-start | bytes 11010048 | tf_op jit(solution)/shard_map/all_to_all | solution.py:77
Sparse Core Ops, SparseCore 0:
  144.7 21.7 reduce-scatter.2
  168.8 21.7 reduce-scatter.4
where the time goes:
time: 359 us
  waiting for transfers between devices  159 us (44%)
  blocking collectives  136 us (38%)
  matrix products  17.8 us (5%)
  between operations  13.5 us (4%)
  other arithmetic  13.3 us (4%)
  local copies, waits for them, and re-layouts  12.9 us (4%)
  starting transfers between devices  7.4 us (2%)
    all_to_all x1, blocking collectives, shards(): lax.all_to_all(outgoing, 'epouter', split_axis=0, concat_axis=0, tiled=True)  127 us
    all_to_all x1, waiting for transfers between devices, shards(): lax.all_to_all(outputs.reshape(outer_size, slot_count, slice_width), 'epo...  120 us
    reduce_scatter x1, waiting for transfers between devices, expert_rows(): lax.psum_scatter(up_part, 'epinner', scatter_dimension=0, tiled=True)  24.1 us
    reduce_scatter x1, waiting for transfers between devices, expert_rows(): lax.psum_scatter(gate_part, 'epinner', scatter_dimension=0, tiled=True)  14.4 us
    all_gather x1, blocking collectives, expert_rows(): lax.all_gather(silu_product(gate_part, up_part), 'epinner', axis=0, tiled...  8.57 us
    gather x2, local copies, waits for them, and re-layouts, combine_rows(): fetched = jnp.take(summed, position, axis=0) * gate_values[:, None]  8.23 us
    dot_general x1, matrix products, expert_rows(): up_part = jnp.dot(token_rows, up_matrix, preferred_element_type=jnp.float32)  7.42 us
    all_to_all x1, starting transfers between devices, shards(): lax.all_to_all(outputs.reshape(outer_size, slot_count, slice_width), 'epo...  7.36 us
  transfers between devices with their start and end apart: 3, of which 3 were waited for; matrix products, arithmetic and copies ran while one was open for 2% of the time, Pallas kernels for 0%

commit v1 on v0

v1 whole, which is shorter than its diff:
```python
import functools

import jax
import jax.numpy as jnp
from jax import lax
from jax.experimental import pallas as pl
from jax.experimental.pallas import tpu as pltpu
from jax.sharding import PartitionSpec as P

SLICES = 4
MESH = pl.DeviceIdType.MESH
F32 = jnp.float32
BF16 = jnp.bfloat16


def tile_of(width):
    return next(t for t in (512, 256, 128) if width % t == 0)


def each_tile(width, tile, body):
    @pl.loop(0, width // tile)
    def _(i):
        body(pl.ds(pl.multiple_of(i * tile, tile), tile))


def layer_kernel(
    experts, inner, slot,
    tokens, ids, ids_t, weight, w_gate, w_up, w_down, out,
    w_in, w_out, outgoing, rows, own, x_send, x_recv, hidden, part, core_recv,
    y_send, y_recv, z_send, returned,
    w_sem, zs, zr, ys, yr, cs, cr, xs, xr, ps, pr, qs, qr, bs, br,
):
    block, width = tokens.shape
    picks = ids.shape[1]
    hid = w_down.shape[1]
    here = lax.axis_index("epouter")
    expert = here // SLICES
    part_at = here % SLICES
    side = part_at % 2
    sib = part_at + 1 - 2 * side
    flip = lax.rem(part_at + 2, SLICES)
    sib_flip = lax.rem(sib + 2, SLICES)
    base = expert * SLICES
    x_at = lax.axis_index("epinner")
    tile = tile_of(width)

    def at_layer(step):
        return {"epouter": lax.rem(expert + step + experts, experts) * SLICES + part_at}

    to_sib = {"epouter": base + sib}
    to_flip = {"epouter": base + flip}

    def at_inner(step):
        return {"epinner": lax.rem(x_at + step, inner)}

    loads = [
        pltpu.make_async_copy(w_gate.at[0], w_in.at[:, pl.ds(0, hid)], w_sem.at[0]),
        pltpu.make_async_copy(w_up.at[0], w_in.at[:, pl.ds(hid, hid)], w_sem.at[1]),
        pltpu.make_async_copy(w_down.at[0], w_out, w_sem.at[2]),
    ]

    barrier = pltpu.get_barrier_semaphore()
    partners = [at_layer(k) for k in range(1, experts)] + [to_sib, to_flip]
    partners += [at_inner(d) for d in range(1, inner)]
    for partner in partners:
        pl.semaphore_signal(barrier, inc=1, device_id=partner, device_id_type=MESH)

    named_row = lax.rem(expert + lax.broadcasted_iota(jnp.int32, (experts, block), 0), experts)
    chosen_row = jnp.zeros((experts, block), F32)
    for p in range(picks):
        chosen_row += (ids_t[p : p + 1, :] == named_row).astype(F32)
    before = (
        lax.broadcasted_iota(jnp.int32, (block, block), 0)
        < lax.broadcasted_iota(jnp.int32, (block, block), 1)
    ).astype(F32)
    pos_row = jnp.dot(
        chosen_row.astype(BF16), before.astype(BF16), preferred_element_type=F32
    )
    pos_row = jnp.where(chosen_row > 0, pos_row, -1.0)
    slots = lax.broadcasted_iota(jnp.int32, (slot, block), 0).astype(F32)

    def placed(k):
        return jnp.where(pos_row[k : k + 1, :] == slots, 1.0, 0.0).astype(BF16)

    def gather_into(k, target):
        place = placed(k)

        def body(cols):
            target[:, cols] = jnp.dot(
                place, tokens[:, cols], preferred_element_type=F32
            ).astype(BF16)

        each_tile(width, tile, body)

    def remote(src, dst, send, recv, device):
        return pltpu.make_async_remote_copy(
            src_ref=src, dst_ref=dst, send_sem=send, recv_sem=recv,
            device_id=device, device_id_type=MESH,
        )

    def z_out(k):
        return remote(
            outgoing.at[k - 1], rows.at[k, part_at], zs.at[k], zr.at[k], at_layer(k)
        )

    def y_out(k):
        mine = rows.at[k, part_at]
        return remote(mine, mine, ys.at[k], yr.at[k], to_flip)

    def core_out(k, which):
        ref = rows.at[k, part_at if which == 0 else flip]
        return remote(ref, ref, cs.at[k, which], cr.at[k, which], to_sib)

    def x_out(k, d):
        return remote(
            x_send.at[k], x_recv.at[k, d - 1], xs.at[k, d - 1], xr.at[k, d - 1], at_inner(d)
        )

    def core_back(k, which):
        return remote(
            part.at[k, sib if which == 0 else sib_flip], core_recv.at[k, which],
            ps.at[k, which], pr.at[k, which], to_sib,
        )

    def y_back(k):
        return remote(y_send.at[k], y_recv.at[k], qs.at[k], qr.at[k], to_flip)

    def z_back(k):
        return remote(z_send.at[k - 1], returned.at[k], bs.at[k], br.at[k], at_layer(-k))

    gather_into(0, rows.at[0, part_at])
    pl.semaphore_wait(barrier, len(partners))
    y_out(0).start()
    core_out(0, 0).start()
    for k in range(1, experts):
        gather_into(k, outgoing.at[k - 1])
        z_out(k).start()
    for load in loads:
        load.start()

    def arrive(k):
        z_out(k).wait_recv()
        y_out(k).start()
        core_out(k, 0).start()

    def up(k):
        y_out(k).wait_recv()
        core_out(k, 1).start()
        if k == 0:
            loads[0].wait()
            loads[1].wait()
        core_out(k, 0).wait_recv()
        core_out(k, 1).wait_recv()

        def body(cols):
            x = rows[k].reshape(SLICES * slot, width)
            value = jnp.dot(x, w_in[:, cols], preferred_element_type=F32)
            own[k, :, cols] = value
            x_send[k, :, cols] = value.astype(BF16)

        each_tile(2 * hid, 256 if (2 * hid) % 256 == 0 else 128, body)
        for d in range(1, inner):
            x_out(k, d).start()

    def down(k):
        for d in range(1, inner):
            x_out(k, d).wait_recv()
        if k == 0:
            loads[2].wait()

        def act(cols):
            upper = pl.ds(pl.multiple_of(cols.start + hid, 128), cols.size)
            gate = own[k, :, cols]
            lift = own[k, :, upper]
            for d in range(inner - 1):
                gate += x_recv[k, d, :, cols].astype(F32)
                lift += x_recv[k, d, :, upper].astype(F32)
            hidden[:, cols] = (gate / (1.0 + jnp.exp(-gate)) * lift).astype(BF16)

        each_tile(hid, 128, act)

        def body(cols):
            value = jnp.dot(hidden[...], w_out[:, cols], preferred_element_type=F32)
            part[k, :, :, cols] = value.astype(BF16).reshape(SLICES, slot, tile)

        each_tile(width, tile, body)
        core_back(k, 1).start()
        core_back(k, 0).start()

    def fold_core(k):
        core_back(k, 1).wait_recv()

        def body(cols):
            y_send[k, :, cols] = (
                part[k, flip, :, cols].astype(F32) + core_recv[k, 1, :, cols].astype(F32)
            ).astype(BF16)

        each_tile(width, tile, body)
        y_back(k).start()

    def fold_y(k):
        core_back(k, 0).wait_recv()
        y_back(k).wait_recv()
        target = returned.at[0] if k == 0 else z_send.at[k - 1]

        def body(cols):
            target[:, cols] = (
                part[k, part_at, :, cols].astype(F32)
                + core_recv[k, 0, :, cols].astype(F32)
                + y_recv[k, :, cols].astype(F32)
            ).astype(BF16)

        each_tile(width, tile, body)
        if k:
            z_back(k).start()

    for t in range(experts + 3):
        if t + 1 < experts:
            arrive(t + 1)
        if t < experts:
            up(t)
        if 0 <= t - 2 < experts:
            fold_core(t - 2)
        if 0 <= t - 3 < experts:
            fold_y(t - 3)
        if 0 <= t - 1 < experts:
            down(t - 1)

    lanes = experts * slot
    named_col = lax.rem(expert + lax.broadcasted_iota(jnp.int32, (block, experts), 1), experts)
    chosen = jnp.zeros((block, experts), F32)
    coef = jnp.zeros((block, experts), F32)
    for p in range(picks):
        same = ids[:, p : p + 1] == named_col
        chosen += same.astype(F32)
        coef += jnp.where(same, weight[:, p : p + 1], 0.0)
    after = (
        lax.broadcasted_iota(jnp.int32, (block, block), 1)
        < lax.broadcasted_iota(jnp.int32, (block, block), 0)
    ).astype(F32)
    pos = jnp.dot(after.astype(BF16), chosen.astype(BF16), preferred_element_type=F32)
    lane = lax.broadcasted_iota(jnp.int32, (block, lanes), 1)
    spread = jnp.zeros((block, lanes), F32)
    for k in range(experts):
        lane_at = (lane - k * slot).astype(F32)
        hit = (pos[:, k : k + 1] == lane_at) & (lane >= k * slot) & (lane < (k + 1) * slot)
        spread += jnp.where(hit, coef[:, k : k + 1], 0.0)
    high = spread.astype(BF16)
    low = (spread - high.astype(F32)).astype(BF16)
    for k in range(1, experts):
        z_back(k).wait_recv()

    def finish(cols):
        back = returned[:, :, cols].reshape(lanes, tile)
        out[:, cols] = (
            jnp.dot(high, back, preferred_element_type=F32)
            + jnp.dot(low, back, preferred_element_type=F32)
        ).astype(BF16)

    each_tile(width, tile, finish)

    for k in range(experts):
        if k:
            z_out(k).wait_send()
            z_back(k).wait_send()
        y_out(k).wait_send()
        y_back(k).wait_send()
        for which in range(2):
            core_out(k, which).wait_send()
            core_back(k, which).wait_send()
        for d in range(1, inner):
            x_out(k, d).wait_send()


def shards(tokens, expert_ids, route_weight, w_gate, w_up, w_down):
    experts = lax.axis_size("epouter") // SLICES
    inner = lax.axis_size("epinner")
    block, width = tokens.shape
    picks = expert_ids.shape[1]
    hid = w_down.shape[1]
    depth = min(block, 3 * block * picks // (2 * experts))
    slot = -(-depth // 16) * 16
    rows = SLICES * slot
    vmem = pl.BlockSpec(memory_space=pltpu.VMEM)
    hbm = pl.BlockSpec(memory_space=pl.ANY)
    dma = pltpu.SemaphoreType.DMA
    others = max(inner - 1, 1)
    total = experts * rows
    return pl.pallas_call(
        functools.partial(layer_kernel, experts, inner, slot),
        out_shape=jax.ShapeDtypeStruct((block, width), BF16),
        in_specs=[vmem] * 4 + [hbm] * 3,
        out_specs=vmem,
        scratch_shapes=[
            pltpu.VMEM((width, 2 * hid), BF16),
            pltpu.VMEM((hid, width), BF16),
            pltpu.VMEM((max(experts - 1, 1), slot, width), BF16),
            pltpu.VMEM((experts, SLICES, slot, width), BF16),
            pltpu.VMEM((experts, rows, 2 * hid), F32),
            pltpu.VMEM((experts, rows, 2 * hid), BF16),
            pltpu.VMEM((experts, others, rows, 2 * hid), BF16),
            pltpu.VMEM((rows, hid), BF16),
            pltpu.VMEM((experts, SLICES, slot, width), BF16),
            pltpu.VMEM((experts, 2, slot, width), BF16),
            pltpu.VMEM((experts, slot, width), BF16),
            pltpu.VMEM((experts, slot, width), BF16),
            pltpu.VMEM((max(experts - 1, 1), slot, width), BF16),
            pltpu.VMEM((experts, slot, width), BF16),
            dma((3,)),
            dma((experts,)), dma((experts,)),
            dma((experts,)), dma((experts,)),
            dma((experts, 2)), dma((experts, 2)),
            dma((experts, others)), dma((experts, others)),
            dma((experts, 2)), dma((experts, 2)),
            dma((experts,)), dma((experts,)),
            dma((experts,)), dma((experts,)),
        ],
        compiler_params=pltpu.CompilerParams(
            collective_id=0, has_side_effects=True, vmem_limit_bytes=52 * 2**20
        ),
        cost_estimate=pl.CostEstimate(
            flops=6 * total * width * hid,
            bytes_accessed=6 * width * hid + 4 * block * width,
            transcendentals=total * hid,
        ),
    )(tokens, expert_ids, expert_ids.T, route_weight, w_gate, w_up, w_down)


def solution(mesh):
    placed = (
        P(("groups", "epouter"), "epinner"),
        P(("groups", "epouter"), None),
        P(("groups", "epouter"), None),
        P("epouter", "epinner", None),
        P("epouter", "epinner", None),
        P("epouter", None, "epinner"),
    )
    return jax.shard_map(
        shards,
        mesh=mesh,
        in_specs=placed,
        out_specs=P(("groups", "epouter"), "epinner"),
        check_vma=False,
    )
```

time: 359 us -> 104 us (0.29)
  the two profiles are of different devices: /device:TPU:13 before, /device:TPU:0 now
where the time goes in v1:
time: 104 us; the launch traced here: 103 us
  Pallas kernels  99.4 us (96%)
  local copies, waits for them, and re-layouts  4 us (4%)
    pallas_call x1, Pallas kernels, shards(): pl.pallas_call(functools.partial(layer_kernel, experts, inner, slot), out...  99.4 us
    unnamed x7, local copies, waits for them, and re-layouts  4 us

profile of v1, /device:TPU:0, one launch (start us, length us, event | category | flops | bytes accessed | tf_op | source)
XLA Modules:
  0.0 103.4 jit_solution(5842098386901780964)
XLA Ops:
  0.0 0.8 copy.8.weight
  0.8 0.8 copy.7.ids
  1.5 0.0 copy-start
  1.5 0.7 copy-done
  2.2 0.0 copy-start.1
  2.2 1.0 copy-done.1
  3.2 99.4 %shard_map.64 = bf16[64,3584]{1,0:T(8,128)(2,1)S(1)} custom-call(bf16[64,3584]{1,0:T(8,128)(2,1)S(1)} %copy-done.1, s32[64,2]{1,0:T(8,128)S(1)} %copy.7.ids, s32[2,64]{1,0:T(2,128)S(1)} %bitcast.1, f32[64,2]{1,0:T(8,128)S(1)} %copy.8.weight, bf16[1,3584,384]{2,1,0:T(8,128)(2,1)} %w_gate.1, bf16[1,3584,384]{2,1,0:T(8,128)(2,1)} %w_up.1, ...), custom_call_target="tpu_custom_call" | custom-call | flops 6341787648 | bytes 9175040 | tf_op jit(solution)/shard_map/pallas_call | solution.py:289
  102.6 0.8 copy.10
Async XLA Ops:
  1.5 0.7 copy-start
  2.2 1.0 copy-start.1
